TPU v7x, 256 devices: a whole 4x4x8 slice. The times are simulated.
256 devices in a mesh: replica: 16 (over z_hi, y, core), fsdp: 16 (over x, z_lo).
Axes of the slice: x: 4, y: 4, z: 8 (z_hi: 2, z_lo: 4; z = z_hi * 4 + z_lo), core: 2. Of those that a mesh axis runs over, the one named last changes fastest.
Arguments:
- tokens: bfloat16 [65536, 8192], P(('replica', 'fsdp')), may hold values from -6 to 6
- hidden_grad: bfloat16 [65536, 448], P(('replica', 'fsdp')), may hold values from -6 to 6
- gate_next: bfloat16 [16, 448, 8192], P('replica', None, 'fsdp'), may hold values from -0.0625 to 0.0625
- up_next: bfloat16 [16, 448, 8192], P('replica', None, 'fsdp'), may hold values from -0.0625 to 0.0625
- inner_gate: bfloat16 [16, 448, 8192], P('replica', None, 'fsdp'), may hold values from -10 to 10
- anchor: float32 [448, 8192], P(None, 'fsdp'), may hold values from -2 to 2
- momentum: float32 [448, 8192], P(None, 'fsdp'), may hold values from -4 to 4
Outputs:
- token_grad: bfloat16 [65536, 8192], P(('replica', 'fsdp'))
- gate_grad: bfloat16 [16, 448, 8192], P('replica', None, 'fsdp')
- up_grad: bfloat16 [16, 448, 8192], P('replica', None, 'fsdp')
- new_anchor: float32 [448, 8192], P(None, 'fsdp')
- new_momentum: float32 [448, 8192], P(None, 'fsdp')
All inputs are finite; a program needn't handle non-finite values. Where the computation divides by a largest or mean magnitude, that divisor is 1e-20 or more.
Results may differ from a plain program's by a relative error of at most 0.023.
Values may be sent and summed in bfloat16 or wider, within the bound.
A program may use at most 128 MiB of HBM per device.

v0:
```python
import jax
import jax.numpy as jnp
from jax import lax
from jax.sharding import PartitionSpec as P

BLOCK = 128


eps_scale = 1e-06
outer_mu = 0.9
outer_rate = 0.7


def contract_last(left, right):
    return lax.dot_general(
        left, right, (((1,), (1,)), ((), ())), preferred_element_type=jnp.float32
    )


def contract_first(left, right):
    return lax.dot_general(
        left, right, (((0,), (0,)), ((), ())), preferred_element_type=jnp.float32
    )


def hidden_cots(gate, upval, cotan):
    cotan = cotan.astype(jnp.float32)
    sig = jax.nn.sigmoid(gate)
    gate_cot = (cotan * upval * sig * (1.0 + gate * (1.0 - sig))).astype(jnp.bfloat16)
    up_cot = (cotan * gate * sig).astype(jnp.bfloat16)
    return (gate_cot, up_cot)


def block_code(anchor, inner):
    delta = anchor - inner.astype(jnp.float32)
    blocks = delta.reshape(delta.shape[0], delta.shape[1] // BLOCK, BLOCK)
    scale = jnp.max(jnp.abs(blocks), axis=-1, keepdims=True) + eps_scale
    code = jnp.floor(blocks / scale * 7.0 + 0.5).astype(jnp.bfloat16)
    return (code, scale)


def nesterov(outer_grad, anchor, momentum):
    new_momentum = outer_mu * momentum + outer_grad
    new_anchor = anchor - outer_rate * (outer_grad + outer_mu * new_momentum)
    return (new_anchor, new_momentum)


def shards(tokens, hidden_grad, gate_next, up_next, inner_gate, anchor, momentum):
    replicas = lax.axis_size("replica")
    gate_full, up_full = (
        lax.all_gather(gate_next, "fsdp", axis=2, tiled=True),
        lax.all_gather(up_next, "fsdp", axis=2, tiled=True),
    )
    gate = contract_last(tokens, gate_full[0])
    upval = contract_last(tokens, up_full[0])
    gate_cot, up_cot = hidden_cots(gate, upval, hidden_grad)
    back = jnp.dot(gate_cot, gate_full[0], preferred_element_type=jnp.float32)
    back = back + jnp.dot(up_cot, up_full[0], preferred_element_type=jnp.float32)
    token_grad = back.astype(jnp.bfloat16)
    gate_term = contract_first(gate_cot, tokens)[None]
    up_term = contract_first(up_cot, tokens)[None]
    gate_sum, up_sum = (
        lax.psum_scatter(
            gate_term.astype(jnp.bfloat16), "fsdp", scatter_dimension=2, tiled=True
        ).astype(jnp.float32),
        lax.psum_scatter(
            up_term.astype(jnp.bfloat16), "fsdp", scatter_dimension=2, tiled=True
        ).astype(jnp.float32),
    )
    gate_grad = gate_sum.astype(jnp.bfloat16)
    up_grad = up_sum.astype(jnp.bfloat16)
    code, scale = block_code(anchor, inner_gate[0])
    decoded = (scale * code.astype(jnp.float32) / 7.0).reshape(anchor.shape)
    total = lax.psum(decoded.astype(jnp.bfloat16), "replica").astype(jnp.float32)
    new_anchor, new_momentum = nesterov(total / replicas, anchor, momentum)
    return (token_grad, gate_grad, up_grad, new_anchor, new_momentum)


def solution(mesh):
    return jax.shard_map(
        shards,
        mesh=mesh,
        in_specs=(
            P(("replica", "fsdp"), None),
            P(("replica", "fsdp"), None),
            P("replica", None, "fsdp"),
            P("replica", None, "fsdp"),
            P("replica", None, "fsdp"),
            P(None, "fsdp"),
            P(None, "fsdp"),
        ),
        out_specs=(
            P(("replica", "fsdp"), None),
            P("replica", None, "fsdp"),
            P("replica", None, "fsdp"),
            P(None, "fsdp"),
            P(None, "fsdp"),
        ),
        check_vma=False,
    )
```

profile of v0, /device:TPU:8, one launch (start us, length us, event | category | flops | bytes accessed | tf_op | source)
XLA Modules:
  0.0 697.0 jit_solution(2892143722401373862)
XLA Ops:
  8.0 0.0 copy-start.2
  8.0 0.0 copy-start.1
  8.0 0.0 all-gather.5.cloned.1.call-start
  8.1 0.7 all-gather.5.cloned.1.call-update
  8.8 0.0 all-gather.3.cloned.1.call-start
  8.8 0.7 all-gather.3.cloned.1.call-update
  9.5 0.0 all-reduce.2.cloned.1.call-start
  9.6 1.4 fusion.28
  11.0 0.3 abs.7
  11.3 0.5 reduce_max.9
  11.9 0.5 mul.51
  12.4 0.0 copy-done.2
  12.4 0.0 copy-done.1
  12.5 1.1 fusion.26
  13.5 0.0 all-reduce.2.cloned.1.call-update
  13.6 0.0 copy-start.3
  13.6 0.0 reduce-scatter.3.cloned.1.call-start
  13.6 164.6 %all-gather.5.cloned.1.call-done = bf16[1,448,8192]{2,1,0:T(8,128)(2,1)} async-done(((bf16[1,448,512]{2,1,0:T(8,128)(2,1)}), bf16[1,448,8192]{2,1,0:T(8,128)(2,1)}) %all-gather.5.cloned.1.call-update) | async-done | bytes 7340048 | tf_op jit(solution)/shard_map/all_gather | solution.py:51
  178.2 6.4 fusion.5
  184.7 161.6 %all-gather.3.cloned.1.call-done = bf16[1,448,8192]{2,1,0:T(8,128)(2,1)} async-done(((bf16[1,448,512]{2,1,0:T(8,128)(2,1)}), bf16[1,448,8192]{2,1,0:T(8,128)(2,1)}) %all-gather.3.cloned.1.call-update) | async-done | bytes 7340048 | tf_op jit(solution)/shard_map/all_gather | solution.py:52
  346.3 0.0 copy-done.3
  346.3 0.0 copy-start
  346.3 6.6 fusion.19
  352.9 0.0 copy-done
  352.9 5.0 fusion
  358.0 0.0 reduce-scatter.3.cloned.1.call-update
  358.0 0.0 copy-start.4
  358.0 0.2 reduce-scatter.5.cloned.1.call-start
  358.2 7.3 %fusion.1 = bf16[1,448,8192]{2,1,0:T(8,128)(2,1)} fusion(bf16[256,8192]{1,0:T(8,128)(2,1)} %param.7, f32[256,448]{0,1:T(8,128)S(1)} %fusion.5, bf16[256,448]{0,1:T(8,128)(2,1)S(1)} %copy-done.3), kind=kOutput, calls=%fused_computation.3 | convolution fusion | flops 1883521024 | bytes 12222464 | tf_op jit(solution)/shard_map/dot_general | solution.py:21
  365.5 0.0 reduce-scatter.5.cloned.1.call-update
  365.5 0.0 all-reduce.2.cloned.1.call-done
  365.6 0.0 copy-done.4
  365.6 0.0 slice-start
  365.6 2.7 multiply_subtract_fusion
  368.3 0.0 slice-start.1
  368.3 5.9 fusion.3
  374.2 0.0 slice-done
  374.2 0.0 slice-done.1
  374.2 4.5 fusion.2
  378.7 145.6 %reduce-scatter.3.cloned.1.call-done = bf16[1,448,512]{2,1,0:T(8,128)(2,1)} async-done(((bf16[1,448,8192]{2,1,0:T(8,128)(2,1)}), bf16[1,448,512]{2,1,0:T(8,128)(2,1)}) %reduce-scatter.3.cloned.1.call-update) | async-done | bytes 458768 | tf_op jit(solution)/shard_map/reduce_scatter | solution.py:63
  524.3 165.6 %reduce-scatter.5.cloned.1.call-done = bf16[1,448,512]{2,1,0:T(8,128)(2,1)} async-done(((bf16[1,448,8192]{2,1,0:T(8,128)(2,1)}), bf16[1,448,512]{2,1,0:T(8,128)(2,1)}) %reduce-scatter.5.cloned.1.call-update) | async-done | bytes 458768 | tf_op jit(solution)/shard_map/reduce_scatter | solution.py:66
  (2 shorter events, 0.0 us)
Async XLA Ops:
  8.0 4.4 copy-start.2
  8.0 4.4 copy-start.1
  8.0 170.2 %all-gather.5.cloned.1.call-start = ((), (), s32[]{:S(2)}) async-start(), calls=%async_computation.3 | async-start | bytes 7798784 | tf_op jit(solution)/shard_map/all_gather | solution.py:51
  8.8 337.5 %all-gather.3.cloned.1.call-start = ((), (), s32[]{:S(2)}) async-start(), calls=%async_computation.2 | async-start | bytes 7798784 | tf_op jit(solution)/shard_map/all_gather | solution.py:52
  9.5 356.1 %all-reduce.2.cloned.1.call-start = ((), (), s32[]{:S(2)}) async-start(), calls=%async_computation.6 | async-start | bytes 917504 | tf_op jit(solution)/shard_map/psum | solution.py:74
  13.6 332.7 %copy-start.3 = (bf16[256,448]{0,1:T(8,128)(2,1)S(1)}, bf16[256,448]{0,1:T(8,128)(2,1)}, u32[]{:S(2)}) copy-start(bf16[256,448]{0,1:T(8,128)(2,1)} %param.8) | copy-start | bytes 688132
  13.6 510.7 %reduce-scatter.3.cloned.1.call-start = ((), (), s32[]{:S(2)}) async-start(), calls=%async_computation.4 | async-start | bytes 7798784 | tf_op jit(solution)/shard_map/reduce_scatter | solution.py:63
  346.3 6.6 copy-start
  358.0 7.6 %copy-start.4 = (f32[448,512]{1,0:T(8,128)S(1)}, f32[448,512]{1,0:T(8,128)}, u32[]{:S(2)}) copy-start(f32[448,512]{1,0:T(8,128)} %param.13) | copy-start | bytes 2752516
  358.0 331.9 %reduce-scatter.5.cloned.1.call-start = ((), (), s32[]{:S(2)}) async-start(), calls=%async_computation.5 | async-start | bytes 7798784 | tf_op jit(solution)/shard_map/reduce_scatter | solution.py:66
  365.6 8.6 %slice-start = ((s8[7340032]{0:T(1024)(128)(4,1)}), s8[4194304]{0:T(1024)(128)(4,1)S(1)}, s32[]{:S(2)}) async-start(s8[7340032]{0:T(1024)(128)(4,1)} %bitcast.50), calls=%async_computation.7 | async-start | bytes 8388608
  368.3 5.9 slice-start.1
Sparse Core Ops, SparseCore 0:
  10.6 167.5 all-gather.4
  180.0 166.2 all-gather.2
  358.1 166.1 reduce-scatter.2
  527.3 162.5 reduce-scatter.4
Sparse Core Ops, SparseCore 1:
  13.7 330.9 all-reduce.1
where the time goes:
time: 698 us; the launch traced here: 697 us
  waiting for transfers between devices  639 us (92%)
  matrix products  35.7 us (5%)
  between operations  15.4 us (2%)
    reduce_scatter x1, waiting for transfers between devices, shards(): lax.psum_scatter(up_term.astype(jnp.bfloat16), 'fsdp', scatter_dimension=...  166 us
    all_gather x1, waiting for transfers between devices, shards(): lax.all_gather(gate_next, 'fsdp', axis=2, tiled=True)  165 us
    all_gather x1, waiting for transfers between devices, shards(): lax.all_gather(up_next, 'fsdp', axis=2, tiled=True)  162 us
    reduce_scatter x1, waiting for transfers between devices, shards(): lax.psum_scatter(gate_term.astype(jnp.bfloat16), 'fsdp', scatter_dimensio...  146 us
  transfers between devices with their start and end apart: 5, of which 4 were waited for; matrix products, arithmetic and copies ran while one was open for 6% of the time, Pallas kernels for 0%

commit v1 on v0

v1 whole, which is shorter than its diff:
```python
import functools
import jax
import jax.numpy as jnp
from jax import lax
from jax.experimental import pallas as pl
from jax.experimental.pallas import tpu as pltpu
from jax.sharding import PartitionSpec as P

MESH = pl.DeviceIdType.MESH
BF16 = jnp.bfloat16
F32 = jnp.float32

EPS = 1e-06
MU = 0.9
RATE = 0.7

T = 256
FF = 448
COLS = 512
QUART = 2048
D = 8192
RUN = 128

BLOCKS = ((0, 128), (128, 128), (256, 128), (384, 64))
GROUPS = ((0, 256), (256, 512), (512, 768), (768, 896))
ROWS = 896
NG = len(GROUPS)
YROWS = 224
YCOLS = 128


def dot_nt(a, b):
    return lax.dot_general(a, b, (((1,), (1,)), ((), ())), preferred_element_type=F32)


def dot_nn(a, b):
    return lax.dot_general(a, b, (((1,), (0,)), ((), ())), preferred_element_type=F32)


def cots(gate, upval, cotan):
    sig = jax.nn.sigmoid(gate)
    gate_cot = cotan * upval * sig * (1.0 + gate * (1.0 - sig))
    up_cot = cotan * gate * sig
    return gate_cot, up_cot


def kernel(
    tokens, hgrad, gate_n, up_n, inner, anchor, momentum,
    tg_out, gg_out, ug_out, na_out, nm_out,
    xq, w, pst, pown, prx, c, ct, tgs, rsi, rso, fin, hg,
    inn, anc, mom, dec, yrx, ysum, zrx, tot,
    w_l, in_l, out_l, tok_s, tok_r, w_s, w_r, p_s, p_r, c_s, c_r, t_s, t_r, g_s, g_r,
    y_s, y_r, zh_s, zh_r, b_s, b_r,
):
    r = lax.axis_index("replica")
    f = lax.axis_index("fsdp")
    x, z = f // 4, f % 4
    zh, y, core = r // 8, (r // 2) % 4, r % 2
    low = z < 2
    end = (z == 0) | (z == 3)
    mid = (z == 1) | (z == 2)
    step = jnp.where(low, 1, -1)
    inward = (r, f + step)
    outward = (r, f - step)

    def xdev(k):
        return (r, ((x + k) % 4) * 4 + z)

    def ydev(dy, dc):
        return (zh * 8 + ((y + dy) % 4) * 2 + (core + dc) % 2, f)

    zpart = ((r + 8) % 16, f)
    ypeers = [(dy, dc) for dy in range(4) for dc in range(2) if (dy, dc) != (0, 0)]

    def colsz(zz):
        return pl.ds(pl.multiple_of(zz * COLS, COLS), COLS)

    def quart(xx):
        return pl.ds(pl.multiple_of(xx * QUART, QUART), QUART)

    w_local = []
    for b, (u0, n) in enumerate(BLOCKS):
        at = 2 * u0
        w_local.append(pltpu.make_async_copy(
            gate_n.at[0, pl.ds(u0, n)], w.at[pl.ds(at, n), colsz(z)], w_l.at[2 * b]))
        w_local.append(pltpu.make_async_copy(
            up_n.at[0, pl.ds(u0, n)], w.at[pl.ds(at + n, n), colsz(z)], w_l.at[2 * b + 1]))
    for q in w_local:
        q.start()
    own_tok = pltpu.make_async_copy(tokens.at[:, quart(x)], xq.at[0], in_l.at[0])
    in_inner = pltpu.make_async_copy(inner.at[0], inn, in_l.at[1])
    in_anchor = pltpu.make_async_copy(anchor, anc, in_l.at[2])
    in_mom = pltpu.make_async_copy(momentum, mom, in_l.at[3])
    in_hg = pltpu.make_async_copy(hgrad, hg, in_l.at[4])
    for q in (own_tok, in_inner, in_anchor, in_mom, in_hg):
        q.start()

    barrier = pltpu.get_barrier_semaphore()

    def greet(dev):
        pl.semaphore_signal(barrier, inc=1, device_id=dev, device_id_type=MESH)

    for k in (1, 2, 3):
        greet(xdev(k))
    greet(inward)

    @pl.when(mid)
    def _():
        greet(outward)

    for dy, dc in ypeers:
        greet(ydev(dy, dc))
    greet(zpart)
    pl.semaphore_wait(barrier, 12 + jnp.where(mid, 1, 0))

    def remote(src, dst, ss, rs, dev):
        return pltpu.make_async_remote_copy(
            src_ref=src, dst_ref=dst, send_sem=ss, recv_sem=rs, device_id=dev, device_id_type=MESH)

    tok = {k: remote(tokens.at[:, quart((x + k) % 4)], xq.at[k], tok_s.at[k], tok_r.at[k], xdev(k))
           for k in (1, 3, 2)}
    for k in (1, 3, 2):
        tok[k].start()

    near_end = jnp.where(low, 0, 3)
    far_mid = jnp.where(low, 2, 1)
    far_end = jnp.where(low, 3, 0)

    def wpiece(g, origin, slot, dev):
        a, b = GROUPS[g]
        ref = w.at[pl.ds(a, b - a), colsz(origin)]
        return remote(ref, ref, w_s.at[g, slot], w_r.at[g, origin], dev)

    def w_own(g):
        wpiece(g, z, 0, inward).start()

        @pl.when(mid)
        def _():
            wpiece(g, z, 1, outward).start()

    def w_wait_local(g):
        w_local[2 * g].wait()
        w_local[2 * g + 1].wait()

    def w_forward(g):
        @pl.when(mid)
        def _():
            wpiece(g, near_end, 2, inward).wait_recv()
            wpiece(g, near_end, 2, inward).start()
            wpiece(g, far_mid, 3, outward).wait_recv()
            wpiece(g, far_mid, 3, outward).start()

        if g + 1 < NG:
            w_wait_local(g + 1)
            w_own(g + 1)

        @pl.when(mid)
        def _():
            wpiece(g, far_end, 4, outward).wait_recv()
            wpiece(g, far_end, 4, outward).start()

        @pl.when(end)
        def _():
            wpiece(g, z + step, 0, inward).wait_recv()
            wpiece(g, far_mid, 0, inward).wait_recv()
            wpiece(g, far_end, 0, inward).wait_recv()

    def w_drain(g):
        wpiece(g, z, 0, inward).wait_send()

        @pl.when(mid)
        def _():
            wpiece(g, z, 1, outward).wait_send()
            wpiece(g, near_end, 2, inward).wait_send()
            wpiece(g, far_mid, 3, outward).wait_send()
            wpiece(g, far_end, 4, outward).wait_send()

    def yslice(ref, yy, cc):
        return ref.at[pl.ds(pl.multiple_of(cc * YROWS, YROWS), YROWS),
                      pl.ds(pl.multiple_of(yy * YCOLS, YCOLS), YCOLS)]

    def yscatter(i):
        dy, dc = ypeers[i]
        slot = dy * 2 + dc
        return remote(yslice(dec, (y + dy) % 4, (core + dc) % 2), yrx.at[slot],
                      y_s.at[slot], y_r.at[slot], ydev(dy, dc))

    def ygather(i):
        dy, dc = ypeers[i]
        slot = dy * 2 + dc
        return remote(yslice(tot, y, core), yslice(tot, y, core), b_s.at[slot], b_r.at[slot], ydev(dy, dc))

    def ygather_in(i):
        dy, dc = ypeers[i]
        slot = dy * 2 + dc
        ref = yslice(tot, (y + 4 - dy) % 4, (core + dc) % 2)
        return remote(ref, ref, b_s.at[slot], b_r.at[slot], ydev(dy, dc))

    zswap = remote(ysum.at[...], zrx.at[...], zh_s.at[0], zh_r.at[0], zpart)

    def outer_decode():
        in_anchor.wait()
        in_inner.wait()
        for j in range(COLS // RUN):
            s = slice(j * RUN, (j + 1) * RUN)
            delta = anc[:, s] - inn[:, s].astype(F32)
            scale = jnp.max(jnp.abs(delta), axis=-1, keepdims=True) + EPS
            code = jnp.floor((delta / scale) * 7.0 + 0.5)
            dec[:, s] = (scale * code / 7.0).astype(BF16)
        for i in range(7):
            yscatter(i).start()

    def outer_sum():
        total = yslice(dec, y, core)[...].astype(F32)
        for i in range(7):
            yscatter(i).wait_recv()
        for i in range(7):
            dy, dc = ypeers[i]
            total = total + yrx[dy * 2 + dc].astype(F32)
        ysum[...] = total
        zswap.start()

    def outer_share():
        zswap.wait_recv()
        yslice(tot, y, core)[...] = ysum[...] + zrx[...]
        for i in range(7):
            ygather(i).start()

    out_na = pltpu.make_async_copy(anc, na_out, out_l.at[0])
    out_nm = pltpu.make_async_copy(mom, nm_out, out_l.at[1])

    def outer_finish():
        in_mom.wait()
        for i in range(7):
            ygather_in(i).wait_recv()
        grad = tot[...] / 16.0
        new_m = MU * mom[...] + grad
        mom[...] = new_m
        anc[...] = anc[...] - RATE * (grad + MU * new_m)
        out_na.start()
        out_nm.start()

    def lanes(g):
        a, b = GROUPS[g]
        return pl.ds(a, b - a)

    def part_copy(g, k):
        return remote(pst.at[k, :, lanes(g)], prx.at[k, :, lanes(g)], p_s.at[g, k], p_r.at[g, k], xdev(4 - k))

    def cot_copy(g, k):
        return remote(c.at[0, :, lanes(g)], c.at[k, :, lanes(g)], c_s.at[g, k], c_r.at[g, k], xdev(k))

    def partials(g):
        a, b = GROUPS[g]
        for k in (2, 1, 3):
            pst[k, :, a:b] = dot_nt(xq[k], w[a:b, :]).astype(BF16)
            part_copy(g, k).start()
        pown[:, a:b] = dot_nt(xq[0], w[a:b, :])

    def owner(g):
        a, b = GROUPS[g]
        for k in (1, 3, 2):
            part_copy(g, k).wait_recv()
        for u0, n in BLOCKS:
            at = 2 * u0
            if not a <= at < b:
                continue
            full = slice(at, at + 2 * n)
            total = pown[:, full]
            for k in (1, 2, 3):
                total = total + prx[k, :, full].astype(F32)
            if n == 128:
                gc, uc = cots(total[:, :n], total[:, n:], hg[:, u0:u0 + n].astype(F32))
                c[0, :, at:at + n] = gc.astype(BF16)
                c[0, :, at + n:at + 2 * n] = uc.astype(BF16)
            else:
                half = hg[:, u0:u0 + n].astype(F32)
                cotan = jnp.concatenate([half, half], axis=1)
                turned = pltpu.roll(total, n, 1)
                first = lax.broadcasted_iota(jnp.int32, total.shape, 1) < n
                gc, uc = cots(jnp.where(first, total, turned), jnp.where(first, turned, total), cotan)
                c[0, :, full] = jnp.where(first, gc, uc).astype(BF16)
        for k in (2, 1, 3):
            cot_copy(g, k).start()

    def gathered(g):
        a, b = GROUPS[g]
        for k in (1, 3, 2):
            cot_copy(g, k).wait_recv()
        for k in range(4):
            ct[a:b, k * T:(k + 1) * T] = c[k, :, a:b].T

    dest_a = jnp.where(low, 3, 0)
    dest_b = jnp.where(low, 2, 1)
    dest_c = jnp.where(z == 0, 1, jnp.where(z == 1, 0, jnp.where(z == 2, 3, 2)))
    dev_c = (r, f + jnp.where(end, step, -step))
    slot_a = jnp.where(end, 0, 3)
    slot_b = jnp.where(end, 1, 4)
    sends = ((dest_a, inward, slot_a, 0), (dest_b, inward, slot_b, 1), (dest_c, dev_c, 2, 3))

    def grad_copy(g, i):
        a, b = GROUPS[g]
        dest, dev, slot, _ = sends[i]
        return remote(rso.at[i, pl.ds(a, b - a)], rsi.at[slot, pl.ds(a, b - a)],
                      g_s.at[g, i], g_r.at[g, slot], dev)

    def grad_in(g, slot):
        a, b = GROUPS[g]
        ref = rsi.at[slot, pl.ds(a, b - a)]
        return remote(ref, ref, g_s.at[g, 0], g_r.at[g, slot], inward)

    def grad_term(g, dest):
        a, b = GROUPS[g]
        return dot_nn(ct[a:b, :], xq[:, :, colsz(dest)].reshape(4 * T, COLS))

    def grad_send(g, i):
        a, b = GROUPS[g]
        dest, _, _, arrives = sends[i]
        rso[i, a:b] = grad_term(g, dest).astype(BF16)

        @pl.when(mid)
        def _():
            grad_in(g, arrives).wait_recv()
            rso[i, a:b] = (rso[i, a:b].astype(F32) + rsi[arrives, a:b].astype(F32)).astype(BF16)

        grad_copy(g, i).start()

    def grad_own(g):
        a, b = GROUPS[g]
        pown2 = grad_term(g, z)
        grad_in(g, 2).wait_recv()
        pown2 = pown2 + rsi[2, a:b].astype(F32)

        @pl.when(mid)
        def _():
            grad_in(g, 4).wait_recv()
            fin[a:b] = (pown2 + rsi[4, a:b].astype(F32)).astype(BF16)

        @pl.when(end)
        def _():
            fin[a:b] = pown2.astype(BF16)

        for i in out_blocks(g):
            fin_out[i].start()

    fin_out = []
    for b, (u0, n) in enumerate(BLOCKS):
        at = 2 * u0
        fin_out.append(pltpu.make_async_copy(
            fin.at[pl.ds(at, n)], gg_out.at[0, pl.ds(u0, n)], out_l.at[3 + 2 * b]))
        fin_out.append(pltpu.make_async_copy(
            fin.at[pl.ds(at + n, n)], ug_out.at[0, pl.ds(u0, n)], out_l.at[4 + 2 * b]))

    def out_blocks(g):
        return (2 * g, 2 * g + 1)

    def tg_copy(k):
        return remote(tgs.at[k], tg_out.at[:, quart(x)], t_s.at[k], t_r.at[k], xdev(4 - k))

    tg_own = pltpu.make_async_copy(tgs.at[0], tg_out.at[:, quart(x)], out_l.at[2])

    def tg_in(k):
        ref = tg_out.at[:, quart((x + k) % 4)]
        return remote(tgs.at[k], ref, t_s.at[k], t_r.at[k], xdev(4 - k))

    def token_grad(k):
        for j in range(4):
            s = slice(j * COLS, (j + 1) * COLS)
            tgs[k, :, s] = dot_nn(c[k], w[:, s]).astype(BF16)
        if k:
            tg_copy(k).start()
        else:
            tg_own.start()

    w_wait_local(0)
    w_own(0)
    outer_decode()
    w_forward(0)
    outer_sum()
    w_forward(1)
    outer_share()
    own_tok.wait()
    in_hg.wait()
    for k in (1, 3, 2):
        tok[k].wait_recv()
    partials(0)
    partials(1)
    w_forward(2)
    partials(2)
    owner(0)
    w_forward(3)
    partials(3)
    owner(1)
    gathered(0)
    for i in range(3):
        @pl.when(end)
        def _():
            grad_send(0, i)
    owner(2)
    owner(3)
    gathered(1)
    for i in range(3):
        @pl.when(end)
        def _():
            grad_send(1, i)
    gathered(2)
    gathered(3)
    for k in (2, 1, 3):
        token_grad(k)
    for g in range(2):
        for i in range(3):
            @pl.when(mid)
            def _():
                grad_send(g, i)
    for i in range(3):
        grad_send(2, i)
    for i in range(3):
        grad_send(3, i)
    token_grad(0)
    outer_finish()
    for g in range(4):
        grad_own(g)

    for k in (1, 3, 2):
        tg_in(k).wait_recv()
    for k in (1, 2, 3):
        tok[k].wait_send()
        tg_copy(k).wait_send()
        for g in range(NG):
            part_copy(g, k).wait_send()
            cot_copy(g, k).wait_send()
    for g in range(NG):
        w_drain(g)
        for i in range(3):
            grad_copy(g, i).wait_send()
    for i in range(7):
        yscatter(i).wait_send()
        ygather(i).wait_send()
    zswap.wait_send()
    tg_own.wait()
    out_na.wait()
    out_nm.wait()
    for q in fin_out:
        q.wait()


def shards(tokens, hidden_grad, gate_next, up_next, inner_gate, anchor, momentum):
    dma = pltpu.SemaphoreType.DMA
    return pl.pallas_call(
        kernel,
        out_shape=(
            jax.ShapeDtypeStruct((T, D), BF16),
            jax.ShapeDtypeStruct((1, FF, COLS), BF16),
            jax.ShapeDtypeStruct((1, FF, COLS), BF16),
            jax.ShapeDtypeStruct((FF, COLS), F32),
            jax.ShapeDtypeStruct((FF, COLS), F32),
        ),
        in_specs=[pl.BlockSpec(memory_space=pl.ANY)] * 7,
        out_specs=[pl.BlockSpec(memory_space=pl.ANY)] * 5,
        scratch_shapes=[
            pltpu.VMEM((4, T, QUART), BF16),
            pltpu.VMEM((ROWS, QUART), BF16),
            pltpu.VMEM((4, T, ROWS), BF16),
            pltpu.VMEM((T, ROWS), F32),
            pltpu.VMEM((4, T, ROWS), BF16),
            pltpu.VMEM((4, T, ROWS), BF16),
            pltpu.VMEM((ROWS, 4 * T), BF16),
            pltpu.VMEM((4, T, QUART), BF16),
            pltpu.VMEM((5, ROWS, COLS), BF16),
            pltpu.VMEM((3, ROWS, COLS), BF16),
            pltpu.VMEM((ROWS, COLS), BF16),
            pltpu.VMEM((T, FF), BF16),
            pltpu.VMEM((FF, COLS), BF16),
            pltpu.VMEM((FF, COLS), F32),
            pltpu.VMEM((FF, COLS), F32),
            pltpu.VMEM((FF, COLS), BF16),
            pltpu.VMEM((8, YROWS, YCOLS), BF16),
            pltpu.VMEM((YROWS, YCOLS), F32),
            pltpu.VMEM((YROWS, YCOLS), F32),
            pltpu.VMEM((FF, COLS), F32),
            dma((8,)),
            dma((5,)),
            dma((11,)),
            dma((4,)), dma((4,)),
            dma((NG, 5)), dma((NG, 4)),
            dma((NG, 4)), dma((NG, 4)),
            dma((NG, 4)), dma((NG, 4)),
            dma((4,)), dma((4,)),
            dma((NG, 3)), dma((NG, 5)),
            dma((8,)), dma((8,)),
            dma((1,)), dma((1,)),
            dma((8,)), dma((8,)),
        ],
        compiler_params=pltpu.CompilerParams(
            collective_id=0, has_side_effects=True, vmem_limit_bytes=60 * 1024 * 1024
        ),
        cost_estimate=pl.CostEstimate(
            flops=11_300_000_000, bytes_accessed=16_000_000, transcendentals=T * FF
        ),
    )(tokens, hidden_grad, gate_next, up_next, inner_gate, anchor, momentum)


def solution(mesh):
    return jax.shard_map(
        shards,
        mesh=mesh,
        in_specs=(
            P(("replica", "fsdp"), None),
            P(("replica", "fsdp"), None),
            P("replica", None, "fsdp"),
            P("replica", None, "fsdp"),
            P("replica", None, "fsdp"),
            P(None, "fsdp"),
            P(None, "fsdp"),
        ),
        out_specs=(
            P(("replica", "fsdp"), None),
            P("replica", None, "fsdp"),
            P("replica", None, "fsdp"),
            P(None, "fsdp"),
            P(None, "fsdp"),
        ),
        check_vma=False,
    )
```

time: 698 us -> 167 us (0.24)
  waiting for transfers between devices: 639 us -> 0 us
  Pallas kernels: 0 us -> 155 us
  matrix products: 35.7 us -> 0 us
  between operations: 15.4 us -> 0.68 us
  local copies, waits for them, and re-layouts: 0.88 us -> 9.97 us
    all_gather x2 -> x0, waiting for transfers between devices: 326 us -> none  [the longest x1 165 us: shards(): lax.all_gather(gate_next, 'fsdp', axis=2, tiled=True)]
    reduce_scatter x2 -> x0, waiting for transfers between devices: 311 us -> none  [the longest x1 166 us: shards(): lax.psum_scatter(up_term.astype(jnp.bfloat16), 'fsdp', scatter_dimension=...]
    pallas_call x0 -> x1, Pallas kernels: none -> 155 us  [shards(): pl.pallas_call(kernel, out_shape=(jax.ShapeDtypeStruct((T, D), BF16), jax...]
    dot_general x6 -> x0, matrix products: 35.7 us -> none  [the longest x2 13.1 us: contract_last(): lax.dot_general(left, right, (((1,), (1,)), ((), ())), preferred_element_...]
    unnamed x14, local copies, waits for them, and re-layouts: 0.03 us -> 9.97 us
  transfers between devices with their start and end apart: 5 -> 0, of which waited for: 4 -> 0; matrix products, arithmetic and copies ran while one was open for 6% -> 0% of each run, Pallas kernels for 0% -> 0%
where the time goes in v1:
time: 167 us; the launch traced here: 166 us
  Pallas kernels  155 us (93%)
  local copies, waits for them, and re-layouts  9.97 us (6%)
    pallas_call x1, Pallas kernels, shards(): pl.pallas_call(kernel, out_shape=(jax.ShapeDtypeStruct((T, D), BF16), jax...  155 us
    unnamed x14, local copies, waits for them, and re-layouts  9.97 us

profile of v1, /device:TPU:8, one launch (start us, length us, event | category | flops | bytes accessed | tf_op | source)
XLA Modules:
  0.0 166.1 jit_solution(12946112939250528930)
XLA Ops:
  0.6 1.8 %copy.12.hgrad = bf16[256,448]{1,0:T(8,128)(2,1)} copy(bf16[256,448]{0,1:T(8,128)(2,1)} %param.8) | data formatting | bytes 458752 | tf_op args[1]
  2.4 155.5 %shard_map.110 = (bf16[256,8192]{1,0:T(8,128)(2,1)}, bf16[1,448,512]{2,1,0:T(8,128)(2,1)}, bf16[1,448,512]{2,1,0:T(8,128)(2,1)}, f32[448,512]{1,0:T(8,128)}, f32[448,512]{1,0:T(8,128)}) custom-call(bf16[256,8192]{1,0:T(8,128)(2,1)} %tokens.1, bf16[256,448]{1,0:T(8,128)(2,1)} %copy.12.hgrad, bf16[1,448,512]{2,1,0:T(8,128)(2,1)} %gate_n.1, ...), custom_call_target="tpu_custom_call" | custom-call | flops 11299999744 | bytes 16000000 | tf_op jit(solution)/shard_map/pallas_call | solution.py:449
  157.9 0.0 copy-start.3
  157.9 0.0 copy-start.2
  157.9 0.0 copy-start.1
  157.9 0.0 copy-start
  157.9 4.8 %copy.18 = bf16[256,8192]{1,0:T(8,128)(2,1)} copy(bf16[256,8192]{1,0:T(8,128)(2,1)} %get-tuple-element.10) | data formatting | bytes 8388608
  162.7 0.0 copy-done.3
  162.7 0.8 copy.19
  163.5 0.0 copy-done.2
  163.5 0.8 copy.20
  164.3 0.0 copy-done.1
  164.3 0.9 copy.21
  165.2 0.0 copy-done
  165.2 0.9 copy.22
Async XLA Ops:
  157.9 4.8 %copy-start.3 = (bf16[1,448,512]{2,1,0:T(8,128)(2,1)S(1)}, bf16[1,448,512]{2,1,0:T(8,128)(2,1)}, u32[]{:S(2)}) copy-start(bf16[1,448,512]{2,1,0:T(8,128)(2,1)} %get-tuple-element.11) | copy-start | bytes 1376260
  157.9 5.6 %copy-start.2 = (bf16[1,448,512]{2,1,0:T(8,128)(2,1)S(1)}, bf16[1,448,512]{2,1,0:T(8,128)(2,1)}, u32[]{:S(2)}) copy-start(bf16[1,448,512]{2,1,0:T(8,128)(2,1)} %get-tuple-element.12) | copy-start | bytes 1376260
  157.9 6.4 %copy-start.1 = (f32[448,512]{1,0:T(8,128)S(1)}, f32[448,512]{1,0:T(8,128)}, u32[]{:S(2)}) copy-start(f32[448,512]{1,0:T(8,128)} %get-tuple-element.13) | copy-start | bytes 2752516
  157.9 7.3 %copy-start = (f32[448,512]{1,0:T(8,128)S(1)}, f32[448,512]{1,0:T(8,128)}, u32[]{:S(2)}) copy-start(f32[448,512]{1,0:T(8,128)} %get-tuple-element.14) | copy-start | bytes 2752516

commit v2 on v1

--- a/solution.py
+++ b/solution.py
@@ -27,6 +27,7 @@
 NG = len(GROUPS)
 YROWS = 224
 YCOLS = 128
+PARTS = 8
 
 
 def dot_nt(a, b):
@@ -47,7 +48,7 @@
 def kernel(
     tokens, hgrad, gate_n, up_n, inner, anchor, momentum,
     tg_out, gg_out, ug_out, na_out, nm_out,
-    xq, w, pst, pown, prx, c, ct, tgs, rsi, rso, fin, hg,
+    xq, w, pst, pown, prx, c, ct, tgs, rsi, rso, fin, hgt, hg,
     inn, anc, mom, dec, yrx, ysum, zrx, tot,
     w_l, in_l, out_l, tok_s, tok_r, w_s, w_r, p_s, p_r, c_s, c_r, t_s, t_r, g_s, g_r,
     y_s, y_r, zh_s, zh_r, b_s, b_r,
@@ -91,7 +92,7 @@
     in_inner = pltpu.make_async_copy(inner.at[0], inn, in_l.at[1])
     in_anchor = pltpu.make_async_copy(anchor, anc, in_l.at[2])
     in_mom = pltpu.make_async_copy(momentum, mom, in_l.at[3])
-    in_hg = pltpu.make_async_copy(hgrad, hg, in_l.at[4])
+    in_hg = pltpu.make_async_copy(hgrad, hgt, in_l.at[4])
     for q in (own_tok, in_inner, in_anchor, in_mom, in_hg):
         q.start()
 
@@ -142,7 +143,7 @@
         w_local[2 * g].wait()
         w_local[2 * g + 1].wait()
 
-    def w_forward(g):
+    def w_near(g):
         @pl.when(mid)
         def _():
             wpiece(g, near_end, 2, inward).wait_recv()
@@ -154,6 +155,7 @@
             w_wait_local(g + 1)
             w_own(g + 1)
 
+    def w_far(g):
         @pl.when(mid)
         def _():
             wpiece(g, far_end, 4, outward).wait_recv()
@@ -250,12 +252,14 @@
     def cot_copy(g, k):
         return remote(c.at[0, :, lanes(g)], c.at[k, :, lanes(g)], c_s.at[g, k], c_r.at[g, k], xdev(k))
 
-    def partials(g):
-        a, b = GROUPS[g]
-        for k in (2, 1, 3):
-            pst[k, :, a:b] = dot_nt(xq[k], w[a:b, :]).astype(BF16)
-            part_copy(g, k).start()
-        pown[:, a:b] = dot_nt(xq[0], w[a:b, :])
+    def partials(g, ks):
+        a, b = GROUPS[g]
+        for k in ks:
+            if k:
+                pst[k, :, a:b] = dot_nt(xq[k], w[a:b, :]).astype(BF16)
+                part_copy(g, k).start()
+            else:
+                pown[:, a:b] = dot_nt(xq[0], w[a:b, :])
 
     def owner(g):
         a, b = GROUPS[g]
@@ -354,78 +358,99 @@
     def out_blocks(g):
         return (2 * g, 2 * g + 1)
 
-    def tg_copy(k):
-        return remote(tgs.at[k], tg_out.at[:, quart(x)], t_s.at[k], t_r.at[k], xdev(4 - k))
+    def tg_cols(xx, h):
+        return pl.ds(pl.multiple_of(xx * QUART + h * (QUART // 2), QUART // 2), QUART // 2)
+
+    def tg_copy(k, h):
+        return remote(tgs.at[k, :, pl.ds(h * (QUART // 2), QUART // 2)], tg_out.at[:, tg_cols(x, h)],
+                      t_s.at[k, h], t_r.at[k, h], xdev(4 - k))
 
     tg_own = pltpu.make_async_copy(tgs.at[0], tg_out.at[:, quart(x)], out_l.at[2])
 
-    def tg_in(k):
-        ref = tg_out.at[:, quart((x + k) % 4)]
-        return remote(tgs.at[k], ref, t_s.at[k], t_r.at[k], xdev(4 - k))
-
-    def token_grad(k):
-        for j in range(4):
+    def tg_in(k, h):
+        return remote(tgs.at[k, :, pl.ds(h * (QUART // 2), QUART // 2)], tg_out.at[:, tg_cols((x + k) % 4, h)],
+                      t_s.at[k, h], t_r.at[k, h], xdev(4 - k))
+
+    def token_grad(k, h):
+        for j in (2 * h, 2 * h + 1):
             s = slice(j * COLS, (j + 1) * COLS)
             tgs[k, :, s] = dot_nn(c[k], w[:, s]).astype(BF16)
         if k:
-            tg_copy(k).start()
-        else:
-            tg_own.start()
+            tg_copy(k, h).start()
 
     w_wait_local(0)
     w_own(0)
     outer_decode()
-    w_forward(0)
+    in_hg.wait()
+    hg[...] = hgt[...].T
+    own_tok.wait()
+    w_near(0)
     outer_sum()
-    w_forward(1)
+    w_far(0)
+    w_near(1)
+    tok[1].wait_recv()
+    tok[3].wait_recv()
+    partials(0, (1, 3, 0))
+    w_far(1)
     outer_share()
-    own_tok.wait()
-    in_hg.wait()
-    for k in (1, 3, 2):
-        tok[k].wait_recv()
-    partials(0)
-    partials(1)
-    w_forward(2)
-    partials(2)
+    w_near(2)
+    tok[2].wait_recv()
+    partials(0, (2,))
+    partials(1, (1, 3, 2, 0))
     owner(0)
-    w_forward(3)
-    partials(3)
+    w_far(2)
+    w_near(3)
+    partials(2, (1, 3, 2, 0))
     owner(1)
+    w_far(3)
+    partials(3, (1, 3, 2, 0))
     gathered(0)
     for i in range(3):
         @pl.when(end)
         def _():
             grad_send(0, i)
     owner(2)
-    owner(3)
     gathered(1)
     for i in range(3):
         @pl.when(end)
         def _():
             grad_send(1, i)
+    owner(3)
+    for i in range(2):
+        @pl.when(mid)
+        def _():
+            grad_send(0, i)
     gathered(2)
     gathered(3)
-    for k in (2, 1, 3):
-        token_grad(k)
-    for g in range(2):
-        for i in range(3):
-            @pl.when(mid)
-            def _():
-                grad_send(g, i)
+    for h in range(2):
+        for k in (2, 1, 3):
+            token_grad(k, h)
+
+    @pl.when(mid)
+    def _():
+        grad_send(0, 2)
+    for i in range(3):
+        @pl.when(mid)
+        def _():
+            grad_send(1, i)
     for i in range(3):
         grad_send(2, i)
     for i in range(3):
         grad_send(3, i)
-    token_grad(0)
+    token_grad(0, 0)
+    token_grad(0, 1)
+    tg_own.start()
     outer_finish()
     for g in range(4):
         grad_own(g)
 
     for k in (1, 3, 2):
-        tg_in(k).wait_recv()
+        for h in range(2):
+            tg_in(k, h).wait_recv()
     for k in (1, 2, 3):
         tok[k].wait_send()
-        tg_copy(k).wait_send()
+        for h in range(2):
+            tg_copy(k, h).wait_send()
         for g in range(NG):
             part_copy(g, k).wait_send()
             cot_copy(g, k).wait_send()
@@ -444,17 +469,34 @@
         q.wait()
 
 
+def results(tg, gg, ug, na, nm, tg_out, gg_out, ug_out, na_out, nm_out, tv, gv, uv, av, mv, in_s, out_s):
+    ways = [(na, av, na_out), (nm, mv, nm_out), (gg, gv, gg_out), (ug, uv, ug_out)]
+    for i in range(PARTS):
+        rows = pl.ds(i * (T // PARTS), T // PARTS)
+        ways.append((tg.at[rows], tv.at[rows], tg_out.at[rows]))
+    ins = [pltpu.make_async_copy(src, via, in_s.at[i]) for i, (src, via, _) in enumerate(ways)]
+    outs = [pltpu.make_async_copy(via, dst, out_s.at[i]) for i, (_, via, dst) in enumerate(ways)]
+    for q in ins:
+        q.start()
+    for q, o in zip(ins, outs):
+        q.wait()
+        o.start()
+    for o in outs:
+        o.wait()
+
+
 def shards(tokens, hidden_grad, gate_next, up_next, inner_gate, anchor, momentum):
     dma = pltpu.SemaphoreType.DMA
-    return pl.pallas_call(
+    shapes = (
+        jax.ShapeDtypeStruct((T, D), BF16),
+        jax.ShapeDtypeStruct((1, FF, COLS), BF16),
+        jax.ShapeDtypeStruct((1, FF, COLS), BF16),
+        jax.ShapeDtypeStruct((FF, COLS), F32),
+        jax.ShapeDtypeStruct((FF, COLS), F32),
+    )
+    outs = pl.pallas_call(
         kernel,
-        out_shape=(
-            jax.ShapeDtypeStruct((T, D), BF16),
-            jax.ShapeDtypeStruct((1, FF, COLS), BF16),
-            jax.ShapeDtypeStruct((1, FF, COLS), BF16),
-            jax.ShapeDtypeStruct((FF, COLS), F32),
-            jax.ShapeDtypeStruct((FF, COLS), F32),
-        ),
+        out_shape=shapes,
         in_specs=[pl.BlockSpec(memory_space=pl.ANY)] * 7,
         out_specs=[pl.BlockSpec(memory_space=pl.ANY)] * 5,
         scratch_shapes=[
@@ -469,6 +511,7 @@
             pltpu.VMEM((5, ROWS, COLS), BF16),
             pltpu.VMEM((3, ROWS, COLS), BF16),
             pltpu.VMEM((ROWS, COLS), BF16),
+            pltpu.VMEM((FF, T), BF16),
             pltpu.VMEM((T, FF), BF16),
             pltpu.VMEM((FF, COLS), BF16),
             pltpu.VMEM((FF, COLS), F32),
@@ -485,7 +528,7 @@
             dma((NG, 5)), dma((NG, 4)),
             dma((NG, 4)), dma((NG, 4)),
             dma((NG, 4)), dma((NG, 4)),
-            dma((4,)), dma((4,)),
+            dma((4, 2)), dma((4, 2)),
             dma((NG, 3)), dma((NG, 5)),
             dma((8,)), dma((8,)),
             dma((1,)), dma((1,)),
@@ -497,7 +540,23 @@
         cost_estimate=pl.CostEstimate(
             flops=11_300_000_000, bytes_accessed=16_000_000, transcendentals=T * FF
         ),
-    )(tokens, hidden_grad, gate_next, up_next, inner_gate, anchor, momentum)
+    )(tokens, hidden_grad.T, gate_next, up_next, inner_gate, anchor, momentum)
+    return pl.pallas_call(
+        results,
+        out_shape=shapes,
+        in_specs=[pl.BlockSpec(memory_space=pl.ANY)] * 5,
+        out_specs=[pl.BlockSpec(memory_space=pl.ANY)] * 5,
+        scratch_shapes=[
+            pltpu.VMEM((T, D), BF16),
+            pltpu.VMEM((1, FF, COLS), BF16),
+            pltpu.VMEM((1, FF, COLS), BF16),
+            pltpu.VMEM((FF, COLS), F32),
+            pltpu.VMEM((FF, COLS), F32),
+            dma((4 + PARTS,)),
+            dma((4 + PARTS,)),
+        ],
+        compiler_params=pltpu.CompilerParams(vmem_limit_bytes=60 * 1024 * 1024),
+    )(*outs)
 
 
 def solution(mesh):

time: 167 us -> 151 us (0.904)
  local copies, waits for them, and re-layouts: 9.97 us -> 0 us
  Pallas kernels: 155 us -> 150 us
    unnamed x14 -> x0, local copies, waits for them, and re-layouts: 9.97 us -> none
    pallas_call x1 -> x2, Pallas kernels: 155 us -> 150 us  [the longest x1 144 us: shards(): pl.pallas_call(kernel, out_shape=shapes, in_specs=[pl.BlockSpec(memory_sp...]
where the time goes in v2:
time: 151 us; the launch traced here: 150 us
  Pallas kernels  150 us (99%)
    pallas_call x1, Pallas kernels, shards(): pl.pallas_call(kernel, out_shape=shapes, in_specs=[pl.BlockSpec(memory_sp...  144 us
    pallas_call x1, Pallas kernels, shards(): pl.pallas_call(results, out_shape=shapes, in_specs=[pl.BlockSpec(memory_s...  5.87 us

profile of v2, /device:TPU:8, one launch (start us, length us, event | category | flops | bytes accessed | tf_op | source)
XLA Modules:
  0.0 150.3 jit_solution(11037350433729382952)
XLA Ops:
  0.6 143.7 %shard_map.110 = (bf16[256,8192]{1,0:T(8,128)(2,1)}, bf16[1,448,512]{2,1,0:T(8,128)(2,1)}, bf16[1,448,512]{2,1,0:T(8,128)(2,1)}, f32[448,512]{1,0:T(8,128)}, f32[448,512]{1,0:T(8,128)}) custom-call(bf16[256,8192]{1,0:T(8,128)(2,1)} %tokens.1, bf16[448,256]{1,0:T(8,128)(2,1)} %bitcast.1, bf16[1,448,512]{2,1,0:T(8,128)(2,1)} %gate_n.1, ...), custom_call_target="tpu_custom_call" | custom-call | flops 11299999744 | bytes 16000000 | tf_op jit(solution)/shard_map/pallas_call | solution.py:497
  144.3 5.9 %shard_map.111 = (bf16[256,8192]{1,0:T(8,128)(2,1)}, bf16[1,448,512]{2,1,0:T(8,128)(2,1)}, bf16[1,448,512]{2,1,0:T(8,128)(2,1)}, f32[448,512]{1,0:T(8,128)}, f32[448,512]{1,0:T(8,128)}) custom-call(bf16[256,8192]{1,0:T(8,128)(2,1)} %get-tuple-element.10.tg, bf16[1,448,512]{2,1,0:T(8,128)(2,1)} %get-tuple-element.11.gg, ...), custom_call_target="tpu_custom_call" | custom-call | tf_op jit(solution)/shard_map/pallas_call | solution.py:544

commit v3 on v2

--- a/solution.py
+++ b/solution.py
@@ -25,6 +25,7 @@
 GROUPS = ((0, 256), (256, 512), (512, 768), (768, 896))
 ROWS = 896
 NG = len(GROUPS)
+RING = (False, True, True, True)
 YROWS = 224
 YCOLS = 128
 PARTS = 8
@@ -48,9 +49,9 @@
 def kernel(
     tokens, hgrad, gate_n, up_n, inner, anchor, momentum,
     tg_out, gg_out, ug_out, na_out, nm_out,
-    xq, w, pst, pown, prx, c, ct, tgs, rsi, rso, fin, hgt, hg,
+    xq, w, pst, pown, phop, prx, c, ct, tgs, rsi, rso, hgt, hg,
     inn, anc, mom, dec, yrx, ysum, zrx, tot,
-    w_l, in_l, out_l, tok_s, tok_r, w_s, w_r, p_s, p_r, c_s, c_r, t_s, t_r, g_s, g_r,
+    w_l, in_l, tok_s, tok_r, w_s, w_r, p_s, p_r, c_s, c_r, t_s, t_r, g_s, g_r,
     y_s, y_r, zh_s, zh_r, b_s, b_r,
 ):
     r = lax.axis_index("replica")
@@ -119,8 +120,8 @@
             src_ref=src, dst_ref=dst, send_sem=ss, recv_sem=rs, device_id=dev, device_id_type=MESH)
 
     tok = {k: remote(tokens.at[:, quart((x + k) % 4)], xq.at[k], tok_s.at[k], tok_r.at[k], xdev(k))
-           for k in (1, 3, 2)}
-    for k in (1, 3, 2):
+           for k in (1, 2, 3)}
+    for k in (2, 1, 3):
         tok[k].start()
 
     near_end = jnp.where(low, 0, 3)
@@ -132,16 +133,22 @@
         ref = w.at[pl.ds(a, b - a), colsz(origin)]
         return remote(ref, ref, w_s.at[g, slot], w_r.at[g, origin], dev)
 
-    def w_own(g):
-        wpiece(g, z, 0, inward).start()
-
-        @pl.when(mid)
-        def _():
-            wpiece(g, z, 1, outward).start()
-
     def w_wait_local(g):
         w_local[2 * g].wait()
         w_local[2 * g + 1].wait()
+
+    def w_start():
+        for g in range(NG):
+            w_wait_local(g)
+
+            @pl.when(end if g else end | mid)
+            def _():
+                wpiece(g, z, 0, inward).start()
+
+            if g == 0:
+                @pl.when(mid)
+                def _():
+                    wpiece(g, z, 1, outward).start()
 
     def w_near(g):
         @pl.when(mid)
@@ -150,10 +157,9 @@
             wpiece(g, near_end, 2, inward).start()
             wpiece(g, far_mid, 3, outward).wait_recv()
             wpiece(g, far_mid, 3, outward).start()
-
-        if g + 1 < NG:
-            w_wait_local(g + 1)
-            w_own(g + 1)
+            if g + 1 < NG:
+                wpiece(g + 1, z, 0, inward).start()
+                wpiece(g + 1, z, 1, outward).start()
 
     def w_far(g):
         @pl.when(mid)
@@ -161,6 +167,7 @@
             wpiece(g, far_end, 4, outward).wait_recv()
             wpiece(g, far_end, 4, outward).start()
 
+    def w_here(g):
         @pl.when(end)
         def _():
             wpiece(g, z + step, 0, inward).wait_recv()
@@ -228,71 +235,122 @@
         for i in range(7):
             ygather(i).start()
 
-    out_na = pltpu.make_async_copy(anc, na_out, out_l.at[0])
-    out_nm = pltpu.make_async_copy(mom, nm_out, out_l.at[1])
-
     def outer_finish():
         in_mom.wait()
         for i in range(7):
             ygather_in(i).wait_recv()
         grad = tot[...] / 16.0
         new_m = MU * mom[...] + grad
-        mom[...] = new_m
-        anc[...] = anc[...] - RATE * (grad + MU * new_m)
-        out_na.start()
-        out_nm.start()
+        nm_out[...] = new_m
+        na_out[...] = anc[...] - RATE * (grad + MU * new_m)
 
     def lanes(g):
         a, b = GROUPS[g]
         return pl.ds(a, b - a)
 
+    lower, upper = pl.ds(0, T // 2), pl.ds(T // 2, T // 2)
+
+    def hop_copy(g, i):
+        rows = (lower, upper)[i]
+        return remote(pst.at[2, rows, lanes(g)], phop.at[rows, lanes(g)],
+                      p_s.at[g, 2 * i], p_r.at[g, 2 * i], xdev((1, 3)[i]))
+
     def part_copy(g, k):
-        return remote(pst.at[k, :, lanes(g)], prx.at[k, :, lanes(g)], p_s.at[g, k], p_r.at[g, k], xdev(4 - k))
+        return remote(pst.at[k, :, lanes(g)], prx.at[k // 2, :, lanes(g)], p_s.at[g, k], p_r.at[g, k], xdev(4 - k))
 
     def cot_copy(g, k):
         return remote(c.at[0, :, lanes(g)], c.at[k, :, lanes(g)], c_s.at[g, k], c_r.at[g, k], xdev(k))
 
-    def partials(g, ks):
-        a, b = GROUPS[g]
-        for k in ks:
-            if k:
-                pst[k, :, a:b] = dot_nt(xq[k], w[a:b, :]).astype(BF16)
-                part_copy(g, k).start()
+    def cot_hop(g, i):
+        rows = (lower, upper)[i]
+        return remote(c.at[(1, 3)[i], rows, lanes(g)], c.at[2, rows, lanes(g)],
+                      c_s.at[g, 2 * i], c_r.at[g, 2 * i], xdev((1, 3)[i]))
+
+    def part_far(g):
+        return remote(pst.at[2, :, lanes(g)], phop.at[:, lanes(g)], p_s.at[g, 0], p_r.at[g, 0], xdev(2))
+
+    def opposite(g):
+        a, b = GROUPS[g]
+        pst[2, :, a:b] = dot_nt(xq[2], w[a:b, :]).astype(BF16)
+        if not RING[g]:
+            part_far(g).start()
+            return
+        for i in range(2):
+            hop_copy(g, i).start()
+
+    def neighbours(g):
+        a, b = GROUPS[g]
+        half = T // 2
+        for i, k in enumerate((3, 1)):
+            rows = slice(i * half, (i + 1) * half)
+            other = slice((1 - i) * half, (2 - i) * half)
+            part = dot_nt(xq[k], w[a:b, :])
+            if RING[g]:
+                hop_copy(g, i).wait_recv()
+                pst[k, rows, a:b] = (part[rows] + phop[rows, a:b].astype(F32)).astype(BF16)
+                pst[k, other, a:b] = part[other].astype(BF16)
             else:
-                pown[:, a:b] = dot_nt(xq[0], w[a:b, :])
+                pst[k, :, a:b] = part.astype(BF16)
+            part_copy(g, k).start()
+
+    def own_part(g):
+        a, b = GROUPS[g]
+        pown[:, a:b] = dot_nt(xq[0], w[a:b, :])
 
     def owner(g):
         a, b = GROUPS[g]
-        for k in (1, 3, 2):
+        for k in (3, 1):
             part_copy(g, k).wait_recv()
+        if not RING[g]:
+            part_far(g).wait_recv()
         for u0, n in BLOCKS:
             at = 2 * u0
             if not a <= at < b:
                 continue
             full = slice(at, at + 2 * n)
-            total = pown[:, full]
-            for k in (1, 2, 3):
-                total = total + prx[k, :, full].astype(F32)
+            total = pown[:, full] + prx[0, :, full].astype(F32) + prx[1, :, full].astype(F32)
+            if not RING[g]:
+                total = total + phop[:, full].astype(F32)
             if n == 128:
                 gc, uc = cots(total[:, :n], total[:, n:], hg[:, u0:u0 + n].astype(F32))
                 c[0, :, at:at + n] = gc.astype(BF16)
                 c[0, :, at + n:at + 2 * n] = uc.astype(BF16)
             else:
-                half = hg[:, u0:u0 + n].astype(F32)
-                cotan = jnp.concatenate([half, half], axis=1)
+                part = hg[:, u0:u0 + n].astype(F32)
+                cotan = jnp.concatenate([part, part], axis=1)
                 turned = pltpu.roll(total, n, 1)
                 first = lax.broadcasted_iota(jnp.int32, total.shape, 1) < n
                 gc, uc = cots(jnp.where(first, total, turned), jnp.where(first, turned, total), cotan)
                 c[0, :, full] = jnp.where(first, gc, uc).astype(BF16)
-        for k in (2, 1, 3):
+        for k in (1, 3) if RING[g] else (2, 1, 3):
             cot_copy(g, k).start()
 
-    def gathered(g):
-        a, b = GROUPS[g]
-        for k in (1, 3, 2):
+    def cot_pass(g):
+        for i, k in enumerate((1, 3)):
             cot_copy(g, k).wait_recv()
+            cot_hop(g, i).start()
+
+    def cot_last(g):
+        if not RING[g]:
+            cot_copy(g, 2).wait_recv()
+            return
+        for i in range(2):
+            cot_hop(g, i).wait_recv()
+
+    def turn(g):
+        a, b = GROUPS[g]
         for k in range(4):
             ct[a:b, k * T:(k + 1) * T] = c[k, :, a:b].T
+
+    def gathered(g):
+        a, b = GROUPS[g]
+        if not RING[g]:
+            for k in (1, 3):
+                cot_copy(g, k).wait_recv()
+        for k in (0, 1, 3):
+            ct[a:b, k * T:(k + 1) * T] = c[k, :, a:b].T
+        cot_last(g)
+        ct[a:b, 2 * T:3 * T] = c[2, :, a:b].T
 
     dest_a = jnp.where(low, 3, 0)
     dest_b = jnp.where(low, 2, 1)
@@ -338,25 +396,19 @@
         @pl.when(mid)
         def _():
             grad_in(g, 4).wait_recv()
-            fin[a:b] = (pown2 + rsi[4, a:b].astype(F32)).astype(BF16)
+            put(g, pown2 + rsi[4, a:b].astype(F32))
 
         @pl.when(end)
         def _():
-            fin[a:b] = pown2.astype(BF16)
-
-        for i in out_blocks(g):
-            fin_out[i].start()
-
-    fin_out = []
-    for b, (u0, n) in enumerate(BLOCKS):
-        at = 2 * u0
-        fin_out.append(pltpu.make_async_copy(
-            fin.at[pl.ds(at, n)], gg_out.at[0, pl.ds(u0, n)], out_l.at[3 + 2 * b]))
-        fin_out.append(pltpu.make_async_copy(
-            fin.at[pl.ds(at + n, n)], ug_out.at[0, pl.ds(u0, n)], out_l.at[4 + 2 * b]))
-
-    def out_blocks(g):
-        return (2 * g, 2 * g + 1)
+            put(g, pown2)
+
+    def put(g, total):
+        a, b = GROUPS[g]
+        for u0, n in BLOCKS:
+            at = 2 * u0 - a
+            if 0 <= at < b - a:
+                gg_out[0, u0:u0 + n] = total[at:at + n].astype(BF16)
+                ug_out[0, u0:u0 + n] = total[at + n:at + 2 * n].astype(BF16)
 
     def tg_cols(xx, h):
         return pl.ds(pl.multiple_of(xx * QUART + h * (QUART // 2), QUART // 2), QUART // 2)
@@ -365,8 +417,6 @@
         return remote(tgs.at[k, :, pl.ds(h * (QUART // 2), QUART // 2)], tg_out.at[:, tg_cols(x, h)],
                       t_s.at[k, h], t_r.at[k, h], xdev(4 - k))
 
-    tg_own = pltpu.make_async_copy(tgs.at[0], tg_out.at[:, quart(x)], out_l.at[2])
-
     def tg_in(k, h):
         return remote(tgs.at[k, :, pl.ds(h * (QUART // 2), QUART // 2)], tg_out.at[:, tg_cols((x + k) % 4, h)],
                       t_s.at[k, h], t_r.at[k, h], xdev(4 - k))
@@ -374,57 +424,78 @@
     def token_grad(k, h):
         for j in (2 * h, 2 * h + 1):
             s = slice(j * COLS, (j + 1) * COLS)
-            tgs[k, :, s] = dot_nn(c[k], w[:, s]).astype(BF16)
+            part = dot_nn(c[k], w[:, s]).astype(BF16)
+            if k:
+                tgs[k, :, s] = part
+            else:
+                tg_out[:, pl.ds(pl.multiple_of(x * QUART + j * COLS, COLS), COLS)] = part
         if k:
             tg_copy(k, h).start()
 
-    w_wait_local(0)
-    w_own(0)
+    w_start()
     outer_decode()
+    w_near(0)
     in_hg.wait()
     hg[...] = hgt[...].T
-    own_tok.wait()
-    w_near(0)
-    outer_sum()
     w_far(0)
     w_near(1)
+    outer_sum()
+    own_tok.wait()
+    w_here(0)
+    tok[2].wait_recv()
+    opposite(0)
+    w_far(1)
+    own_part(0)
+    w_near(2)
+    outer_share()
+    w_far(2)
+    w_near(3)
+    w_here(1)
+    own_part(1)
+    outer_finish()
+    w_far(3)
     tok[1].wait_recv()
     tok[3].wait_recv()
-    partials(0, (1, 3, 0))
-    w_far(1)
-    outer_share()
-    w_near(2)
-    tok[2].wait_recv()
-    partials(0, (2,))
-    partials(1, (1, 3, 2, 0))
+    neighbours(0)
+    opposite(1)
     owner(0)
-    w_far(2)
-    w_near(3)
-    partials(2, (1, 3, 2, 0))
-    owner(1)
-    w_far(3)
-    partials(3, (1, 3, 2, 0))
+    neighbours(1)
+    w_here(2)
+    opposite(2)
+    own_part(2)
     gathered(0)
     for i in range(3):
         @pl.when(end)
         def _():
             grad_send(0, i)
+    w_here(3)
+    opposite(3)
+    own_part(3)
+    owner(1)
+    neighbours(2)
+    neighbours(3)
+    cot_pass(1)
     owner(2)
+    owner(3)
     gathered(1)
     for i in range(3):
         @pl.when(end)
         def _():
             grad_send(1, i)
-    owner(3)
     for i in range(2):
         @pl.when(mid)
         def _():
             grad_send(0, i)
-    gathered(2)
-    gathered(3)
-    for h in range(2):
-        for k in (2, 1, 3):
-            token_grad(k, h)
+    cot_pass(2)
+    cot_pass(3)
+    cot_last(2)
+    token_grad(1, 0)
+    token_grad(3, 0)
+    cot_last(3)
+    for k, h in ((2, 0), (2, 1), (1, 1), (3, 1)):
+        token_grad(k, h)
+    turn(2)
+    turn(3)
 
     @pl.when(mid)
     def _():
@@ -439,8 +510,6 @@
         grad_send(3, i)
     token_grad(0, 0)
     token_grad(0, 1)
-    tg_own.start()
-    outer_finish()
     for g in range(4):
         grad_own(g)
 
@@ -452,34 +521,33 @@
         for h in range(2):
             tg_copy(k, h).wait_send()
         for g in range(NG):
-            part_copy(g, k).wait_send()
-            cot_copy(g, k).wait_send()
+            if k != 2:
+                part_copy(g, k).wait_send()
+                cot_copy(g, k).wait_send()
     for g in range(NG):
         w_drain(g)
+        if RING[g]:
+            for i in range(2):
+                hop_copy(g, i).wait_send()
+                cot_hop(g, i).wait_send()
+        else:
+            part_far(g).wait_send()
+            cot_copy(g, 2).wait_send()
         for i in range(3):
             grad_copy(g, i).wait_send()
     for i in range(7):
         yscatter(i).wait_send()
         ygather(i).wait_send()
     zswap.wait_send()
-    tg_own.wait()
-    out_na.wait()
-    out_nm.wait()
-    for q in fin_out:
-        q.wait()
-
-
-def results(tg, gg, ug, na, nm, tg_out, gg_out, ug_out, na_out, nm_out, tv, gv, uv, av, mv, in_s, out_s):
-    ways = [(na, av, na_out), (nm, mv, nm_out), (gg, gv, gg_out), (ug, uv, ug_out)]
+
+
+def results(tg, gg, ug, na, nm, tg_out, gg_out, ug_out, na_out, nm_out, out_s):
+    ways = [(na, na_out), (nm, nm_out), (gg, gg_out), (ug, ug_out)]
     for i in range(PARTS):
         rows = pl.ds(i * (T // PARTS), T // PARTS)
-        ways.append((tg.at[rows], tv.at[rows], tg_out.at[rows]))
-    ins = [pltpu.make_async_copy(src, via, in_s.at[i]) for i, (src, via, _) in enumerate(ways)]
-    outs = [pltpu.make_async_copy(via, dst, out_s.at[i]) for i, (_, via, dst) in enumerate(ways)]
-    for q in ins:
-        q.start()
-    for q, o in zip(ins, outs):
-        q.wait()
+        ways.append((tg.at[rows], tg_out.at[rows]))
+    outs = [pltpu.make_async_copy(src, dst, out_s.at[i]) for i, (src, dst) in enumerate(ways)]
+    for o in outs:
         o.start()
     for o in outs:
         o.wait()
@@ -496,21 +564,21 @@
     )
     outs = pl.pallas_call(
         kernel,
-        out_shape=shapes,
-        in_specs=[pl.BlockSpec(memory_space=pl.ANY)] * 7,
-        out_specs=[pl.BlockSpec(memory_space=pl.ANY)] * 5,
+        out_shape=tuple(pltpu.VMEM(o.shape, o.dtype) for o in shapes),
+        in_specs=[pl.BlockSpec(memory_space=pltpu.HBM)] * 7,
+        out_specs=[pl.BlockSpec(memory_space=pltpu.VMEM)] * 5,
         scratch_shapes=[
             pltpu.VMEM((4, T, QUART), BF16),
             pltpu.VMEM((ROWS, QUART), BF16),
             pltpu.VMEM((4, T, ROWS), BF16),
             pltpu.VMEM((T, ROWS), F32),
-            pltpu.VMEM((4, T, ROWS), BF16),
+            pltpu.VMEM((T, ROWS), BF16),
+            pltpu.VMEM((2, T, ROWS), BF16),
             pltpu.VMEM((4, T, ROWS), BF16),
             pltpu.VMEM((ROWS, 4 * T), BF16),
             pltpu.VMEM((4, T, QUART), BF16),
             pltpu.VMEM((5, ROWS, COLS), BF16),
             pltpu.VMEM((3, ROWS, COLS), BF16),
-            pltpu.VMEM((ROWS, COLS), BF16),
             pltpu.VMEM((FF, T), BF16),
             pltpu.VMEM((T, FF), BF16),
             pltpu.VMEM((FF, COLS), BF16),
@@ -523,7 +591,6 @@
             pltpu.VMEM((FF, COLS), F32),
             dma((8,)),
             dma((5,)),
-            dma((11,)),
             dma((4,)), dma((4,)),
             dma((NG, 5)), dma((NG, 4)),
             dma((NG, 4)), dma((NG, 4)),
@@ -535,7 +602,7 @@
             dma((8,)), dma((8,)),
         ],
         compiler_params=pltpu.CompilerParams(
-            collective_id=0, has_side_effects=True, vmem_limit_bytes=60 * 1024 * 1024
+            collective_id=0, has_side_effects=True, vmem_limit_bytes=54 * 1024 * 1024
         ),
         cost_estimate=pl.CostEstimate(
             flops=11_300_000_000, bytes_accessed=16_000_000, transcendentals=T * FF
@@ -544,18 +611,10 @@
     return pl.pallas_call(
         results,
         out_shape=shapes,
-        in_specs=[pl.BlockSpec(memory_space=pl.ANY)] * 5,
+        in_specs=[pl.BlockSpec(memory_space=pltpu.VMEM)] * 5,
         out_specs=[pl.BlockSpec(memory_space=pl.ANY)] * 5,
-        scratch_shapes=[
-            pltpu.VMEM((T, D), BF16),
-            pltpu.VMEM((1, FF, COLS), BF16),
-            pltpu.VMEM((1, FF, COLS), BF16),
-            pltpu.VMEM((FF, COLS), F32),
-            pltpu.VMEM((FF, COLS), F32),
-            dma((4 + PARTS,)),
-            dma((4 + PARTS,)),
-        ],
-        compiler_params=pltpu.CompilerParams(vmem_limit_bytes=60 * 1024 * 1024),
+        scratch_shapes=[dma((4 + PARTS,))],
+        compiler_params=pltpu.CompilerParams(vmem_limit_bytes=16 * 1024 * 1024),
     )(*outs)
 
 

time: 151 us -> 151 us (level)
  the two profiles are of different devices: /device:TPU:8 before, /device:TPU:32 now
where the time goes in v3:
time: 151 us
  Pallas kernels  150 us (99%)
    pallas_call x1, Pallas kernels, shards(): pl.pallas_call(kernel, out_shape=tuple((pltpu.VMEM(o.shape, o.dtype) for...  147 us

profile of v3, /device:TPU:32, one launch (start us, length us, event | category | flops | bytes accessed | tf_op | source)
XLA Modules:
  0.0 150.6 jit_solution(1942098181079040448)
XLA Ops:
  0.6 146.8 %shard_map.110 = (bf16[256,8192]{1,0:T(8,128)(2,1)S(1)}, bf16[1,448,512]{2,1,0:T(8,128)(2,1)S(1)}, bf16[1,448,512]{2,1,0:T(8,128)(2,1)S(1)}, f32[448,512]{1,0:T(8,128)S(1)}, f32[448,512]{1,0:T(8,128)S(1)}) custom-call(bf16[256,8192]{1,0:T(8,128)(2,1)} %tokens.1, bf16[448,256]{1,0:T(8,128)(2,1)} %bitcast.1, bf16[1,448,512]{2,1,0:T(8,128)(2,1)} %gate_n.1, ...), custom_call_target="tpu_custom_call" | custom-call | flops 11299999744 | bytes 16000000 | tf_op jit(solution)/shard_map/pallas_call | solution.py:565
  147.5 3.0 %shard_map.111 = (bf16[256,8192]{1,0:T(8,128)(2,1)}, bf16[1,448,512]{2,1,0:T(8,128)(2,1)}, bf16[1,448,512]{2,1,0:T(8,128)(2,1)}, f32[448,512]{1,0:T(8,128)}, f32[448,512]{1,0:T(8,128)}) custom-call(bf16[256,8192]{1,0:T(8,128)(2,1)S(1)} %get-tuple-element.10.tg, bf16[1,448,512]{2,1,0:T(8,128)(2,1)S(1)} %get-tuple-element.11.gg, ...), custom_call_target="tpu_custom_call" | custom-call | tf_op jit(solution)/shard_map/pallas_call | solution.py:611

commit v4 on v3

--- a/solution.py
+++ b/solution.py
@@ -80,6 +80,22 @@
     def quart(xx):
         return pl.ds(pl.multiple_of(xx * QUART, QUART), QUART)
 
+    barrier = pltpu.get_barrier_semaphore()
+
+    def greet(dev):
+        pl.semaphore_signal(barrier, inc=1, device_id=dev, device_id_type=MESH)
+
+    for k in (1, 2, 3):
+        greet(xdev(k))
+    greet(inward)
+
+    @pl.when(mid)
+    def _():
+        greet(outward)
+
+    for dy, dc in ypeers:
+        greet(ydev(dy, dc))
+    greet(zpart)
     w_local = []
     for b, (u0, n) in enumerate(BLOCKS):
         at = 2 * u0
@@ -97,22 +113,6 @@
     for q in (own_tok, in_inner, in_anchor, in_mom, in_hg):
         q.start()
 
-    barrier = pltpu.get_barrier_semaphore()
-
-    def greet(dev):
-        pl.semaphore_signal(barrier, inc=1, device_id=dev, device_id_type=MESH)
-
-    for k in (1, 2, 3):
-        greet(xdev(k))
-    greet(inward)
-
-    @pl.when(mid)
-    def _():
-        greet(outward)
-
-    for dy, dc in ypeers:
-        greet(ydev(dy, dc))
-    greet(zpart)
     pl.semaphore_wait(barrier, 12 + jnp.where(mid, 1, 0))
 
     def remote(src, dst, ss, rs, dev):
@@ -438,8 +438,8 @@
     in_hg.wait()
     hg[...] = hgt[...].T
     w_far(0)
+    outer_sum()
     w_near(1)
-    outer_sum()
     own_tok.wait()
     w_here(0)
     tok[2].wait_recv()
@@ -447,12 +447,10 @@
     w_far(1)
     own_part(0)
     w_near(2)
-    outer_share()
     w_far(2)
     w_near(3)
     w_here(1)
     own_part(1)
-    outer_finish()
     w_far(3)
     tok[1].wait_recv()
     tok[3].wait_recv()
@@ -471,6 +469,7 @@
     w_here(3)
     opposite(3)
     own_part(3)
+    outer_share()
     owner(1)
     neighbours(2)
     neighbours(3)
@@ -510,6 +509,7 @@
         grad_send(3, i)
     token_grad(0, 0)
     token_grad(0, 1)
+    outer_finish()
     for g in range(4):
         grad_own(g)
 

time: 151 us -> 144 us (0.954)
  the two profiles are of different devices: /device:TPU:32 before, /device:TPU:8 now
where the time goes in v4:
time: 144 us
  Pallas kernels  143 us (99%)
    pallas_call x1, Pallas kernels, shards(): pl.pallas_call(kernel, out_shape=tuple((pltpu.VMEM(o.shape, o.dtype) for...  140 us
    pallas_call x1, Pallas kernels, shards(): pl.pallas_call(results, out_shape=shapes, in_specs=[pl.BlockSpec(memory_s...  2.95 us

profile of v4, /device:TPU:8, one launch (start us, length us, event | category | flops | bytes accessed | tf_op | source)
XLA Modules:
  0.0 143.9 jit_solution(12606717051241454193)
XLA Ops:
  0.6 140.1 %shard_map.110 = (bf16[256,8192]{1,0:T(8,128)(2,1)S(1)}, bf16[1,448,512]{2,1,0:T(8,128)(2,1)S(1)}, bf16[1,448,512]{2,1,0:T(8,128)(2,1)S(1)}, f32[448,512]{1,0:T(8,128)S(1)}, f32[448,512]{1,0:T(8,128)S(1)}) custom-call(bf16[256,8192]{1,0:T(8,128)(2,1)} %tokens.1, bf16[448,256]{1,0:T(8,128)(2,1)} %bitcast.1, bf16[1,448,512]{2,1,0:T(8,128)(2,1)} %gate_n.1, ...), custom_call_target="tpu_custom_call" | custom-call | flops 11299999744 | bytes 16000000 | tf_op jit(solution)/shard_map/pallas_call | solution.py:565
  140.8 3.0 %shard_map.111 = (bf16[256,8192]{1,0:T(8,128)(2,1)}, bf16[1,448,512]{2,1,0:T(8,128)(2,1)}, bf16[1,448,512]{2,1,0:T(8,128)(2,1)}, f32[448,512]{1,0:T(8,128)}, f32[448,512]{1,0:T(8,128)}) custom-call(bf16[256,8192]{1,0:T(8,128)(2,1)S(1)} %get-tuple-element.10.tg, bf16[1,448,512]{2,1,0:T(8,128)(2,1)S(1)} %get-tuple-element.11.gg, ...), custom_call_target="tpu_custom_call" | custom-call | tf_op jit(solution)/shard_map/pallas_call | solution.py:611

commit v5 on v4

--- a/solution.py
+++ b/solution.py
@@ -52,7 +52,7 @@
     xq, w, pst, pown, phop, prx, c, ct, tgs, rsi, rso, hgt, hg,
     inn, anc, mom, dec, yrx, ysum, zrx, tot,
     w_l, in_l, tok_s, tok_r, w_s, w_r, p_s, p_r, c_s, c_r, t_s, t_r, g_s, g_r,
-    y_s, y_r, zh_s, zh_r, b_s, b_r,
+    y_s, y_r, zh_s, zh_r, b_s, b_r, here,
 ):
     r = lax.axis_index("replica")
     f = lax.axis_index("fsdp")
@@ -93,9 +93,20 @@
     def _():
         greet(outward)
 
+    place = r % 8
+
+    def yplace(dy, dc):
+        return ((y + dy) % 4) * 2 + (core + dc) % 2
+
     for dy, dc in ypeers:
-        greet(ydev(dy, dc))
-    greet(zpart)
+        @pl.when(yplace(dy, dc) > place)
+        def _():
+            greet(ydev(dy, dc))
+
+    @pl.when(zh == 0)
+    def _():
+        greet(zpart)
+
     w_local = []
     for b, (u0, n) in enumerate(BLOCKS):
         at = 2 * u0
@@ -113,7 +124,7 @@
     for q in (own_tok, in_inner, in_anchor, in_mom, in_hg):
         q.start()
 
-    pl.semaphore_wait(barrier, 12 + jnp.where(mid, 1, 0))
+    pl.semaphore_wait(barrier, 4 + jnp.where(mid, 1, 0) + place + zh)
 
     def remote(src, dst, ss, rs, dev):
         return pltpu.make_async_remote_copy(
@@ -206,6 +217,27 @@
         return remote(ref, ref, b_s.at[slot], b_r.at[slot], ydev(dy, dc))
 
     zswap = remote(ysum.at[...], zrx.at[...], zh_s.at[0], zh_r.at[0], zpart)
+
+    def answer(dev):
+        pl.semaphore_signal(here, inc=1, device_id=dev, device_id_type=MESH)
+
+    def outer_answer():
+        for dy, dc in ypeers:
+            @pl.when(yplace(dy, dc) < place)
+            def _():
+                answer(ydev(dy, dc))
+
+        @pl.when(zh == 1)
+        def _():
+            answer(zpart)
+
+    def outer_scatter():
+        @pl.when(r < 15)
+        def _():
+            pl.semaphore_wait(here, 8 - place - zh)
+
+        for i in range(7):
+            yscatter(i).start()
 
     def outer_decode():
         in_anchor.wait()
@@ -216,8 +248,6 @@
             scale = jnp.max(jnp.abs(delta), axis=-1, keepdims=True) + EPS
             code = jnp.floor((delta / scale) * 7.0 + 0.5)
             dec[:, s] = (scale * code / 7.0).astype(BF16)
-        for i in range(7):
-            yscatter(i).start()
 
     def outer_sum():
         total = yslice(dec, y, core)[...].astype(F32)
@@ -433,13 +463,14 @@
             tg_copy(k, h).start()
 
     w_start()
+    outer_answer()
     outer_decode()
     w_near(0)
     in_hg.wait()
     hg[...] = hgt[...].T
     w_far(0)
-    outer_sum()
     w_near(1)
+    outer_scatter()
     own_tok.wait()
     w_here(0)
     tok[2].wait_recv()
@@ -448,6 +479,7 @@
     own_part(0)
     w_near(2)
     w_far(2)
+    outer_sum()
     w_near(3)
     w_here(1)
     own_part(1)
@@ -600,6 +632,7 @@
             dma((8,)), dma((8,)),
             dma((1,)), dma((1,)),
             dma((8,)), dma((8,)),
+            pltpu.SemaphoreType.REGULAR,
         ],
         compiler_params=pltpu.CompilerParams(
             collective_id=0, has_side_effects=True, vmem_limit_bytes=54 * 1024 * 1024

time: 144 us -> 142 us (0.986)
  Pallas kernels: 143 us -> 141 us
    pallas_call x1, Pallas kernels: 140 us -> 138 us  [shards(): pl.pallas_call(kernel, out_shape=tuple((pltpu.VMEM(o.shape, o.dtype) for...]
where the time goes in v5:
time: 142 us
  Pallas kernels  141 us (99%)
    pallas_call x1, Pallas kernels, shards(): pl.pallas_call(kernel, out_shape=tuple((pltpu.VMEM(o.shape, o.dtype) for...  138 us
    pallas_call x1, Pallas kernels, shards(): pl.pallas_call(results, out_shape=shapes, in_specs=[pl.BlockSpec(memory_s...  2.95 us

profile of v5, /device:TPU:8, one launch (start us, length us, event | category | flops | bytes accessed | tf_op | source)
XLA Modules:
  0.0 141.8 jit_solution(11221096424223658115)
XLA Ops:
  0.6 138.0 %shard_map.110 = (bf16[256,8192]{1,0:T(8,128)(2,1)S(1)}, bf16[1,448,512]{2,1,0:T(8,128)(2,1)S(1)}, bf16[1,448,512]{2,1,0:T(8,128)(2,1)S(1)}, f32[448,512]{1,0:T(8,128)S(1)}, f32[448,512]{1,0:T(8,128)S(1)}) custom-call(bf16[256,8192]{1,0:T(8,128)(2,1)} %tokens.1, bf16[448,256]{1,0:T(8,128)(2,1)} %bitcast.1, bf16[1,448,512]{2,1,0:T(8,128)(2,1)} %gate_n.1, ...), custom_call_target="tpu_custom_call" | custom-call | flops 11299999744 | bytes 16000000 | tf_op jit(solution)/shard_map/pallas_call | solution.py:597
  138.7 3.0 %shard_map.111 = (bf16[256,8192]{1,0:T(8,128)(2,1)}, bf16[1,448,512]{2,1,0:T(8,128)(2,1)}, bf16[1,448,512]{2,1,0:T(8,128)(2,1)}, f32[448,512]{1,0:T(8,128)}, f32[448,512]{1,0:T(8,128)}) custom-call(bf16[256,8192]{1,0:T(8,128)(2,1)S(1)} %get-tuple-element.10.tg, bf16[1,448,512]{2,1,0:T(8,128)(2,1)S(1)} %get-tuple-element.11.gg, ...), custom_call_target="tpu_custom_call" | custom-call | tf_op jit(solution)/shard_map/pallas_call | solution.py:644

commit v6 on v5

--- a/solution.py
+++ b/solution.py
@@ -535,15 +535,17 @@
         @pl.when(mid)
         def _():
             grad_send(1, i)
-    for i in range(3):
-        grad_send(2, i)
-    for i in range(3):
-        grad_send(3, i)
     token_grad(0, 0)
     token_grad(0, 1)
     outer_finish()
-    for g in range(4):
-        grad_own(g)
+    for i in range(3):
+        grad_send(2, i)
+    grad_own(0)
+    grad_own(1)
+    for i in range(3):
+        grad_send(3, i)
+    grad_own(2)
+    grad_own(3)
 
     for k in (1, 3, 2):
         for h in range(2):

time: 142 us -> 142 us (level)
  no operation moved by 1% of the time
where the time goes in v6:
time: 142 us
  Pallas kernels  141 us (99%)
    pallas_call x1, Pallas kernels, shards(): pl.pallas_call(kernel, out_shape=tuple((pltpu.VMEM(o.shape, o.dtype) for...  138 us
    pallas_call x1, Pallas kernels, shards(): pl.pallas_call(results, out_shape=shapes, in_specs=[pl.BlockSpec(memory_s...  2.95 us

profile of v6, /device:TPU:8, one launch (start us, length us, event | category | flops | bytes accessed | tf_op | source)
XLA Modules:
  0.0 141.8 jit_solution(6995918752861181571)
XLA Ops:
  0.6 138.0 %shard_map.110 = (bf16[256,8192]{1,0:T(8,128)(2,1)S(1)}, bf16[1,448,512]{2,1,0:T(8,128)(2,1)S(1)}, bf16[1,448,512]{2,1,0:T(8,128)(2,1)S(1)}, f32[448,512]{1,0:T(8,128)S(1)}, f32[448,512]{1,0:T(8,128)S(1)}) custom-call(bf16[256,8192]{1,0:T(8,128)(2,1)} %tokens.1, bf16[448,256]{1,0:T(8,128)(2,1)} %bitcast.1, bf16[1,448,512]{2,1,0:T(8,128)(2,1)} %gate_n.1, ...), custom_call_target="tpu_custom_call" | custom-call | flops 11299999744 | bytes 16000000 | tf_op jit(solution)/shard_map/pallas_call | solution.py:599
  138.7 3.0 %shard_map.111 = (bf16[256,8192]{1,0:T(8,128)(2,1)}, bf16[1,448,512]{2,1,0:T(8,128)(2,1)}, bf16[1,448,512]{2,1,0:T(8,128)(2,1)}, f32[448,512]{1,0:T(8,128)}, f32[448,512]{1,0:T(8,128)}) custom-call(bf16[256,8192]{1,0:T(8,128)(2,1)S(1)} %get-tuple-element.10.tg, bf16[1,448,512]{2,1,0:T(8,128)(2,1)S(1)} %get-tuple-element.11.gg, ...), custom_call_target="tpu_custom_call" | custom-call | tf_op jit(solution)/shard_map/pallas_call | solution.py:646
